TPU v7x, 128 devices: a whole 4x4x4 slice. The times are simulated.
128 devices in a mesh: db: 16 (over y, x), seq: 8 (over z, core).
Axes of the slice: x: 4, y: 4, z: 4, core: 2. Of those that a mesh axis runs over, the one named last changes fastest.
Arguments:
- self_query: bfloat16 [49152, 2048], P(('db', 'seq')), may hold values from -500 to 500
- self_key: bfloat16 [49152, 2048], P(('db', 'seq')), may hold values from -6 to 6
- self_value: bfloat16 [49152, 2048], P(('db', 'seq')), may hold values from -6 to 6
- cross_query: bfloat16 [49152, 2048], P(('db', 'seq')), may hold values from -700 to 700
- retrieval_shard: int32 [768, 2], P(('db', 'seq')), may hold values from 0 to 15, all different within a row; in each aligned block of 6 rows (0 to 5, 6 to 11, ...) at most 2 rows name the same one
- retrieval_row: int32 [768, 2], P(('db', 'seq')), may hold values from 0 to 31
- database: bfloat16 [512, 64, 896], P('db'), may hold values from -6 to 6
- ffn_in: bfloat16 [896, 3584], P(None, 'db'), may hold values from -0.1875 to 0.1875
- ffn_out: bfloat16 [3584, 896], P('db'), may hold values from -0.09375 to 0.09375
- cross_projection: bfloat16 [896, 4096], P(None, 'db'), may hold values from -0.1875 to 0.1875
Outputs:
- self_attended: bfloat16 [49152, 2048], P(('db', 'seq'))
- cross_attended: bfloat16 [49152, 2048], P(('db', 'seq'))
Inputs may be any that keep to these rules, and one draw needn't show every extreme that they name: `retrieval_shard`: each row names 2 different shards; among the rows of one device no shard is named more than 2 times, a bound that some block reaches.
All inputs are finite; a program needn't handle non-finite values.
Results may differ from a plain program's by a relative error of at most 0.04.
Values may be sent and summed in bfloat16 or wider, within the bound.
No kernel may reach another device: no remote copies, remote signals or barrier semaphores. Data moves between devices by JAX's collectives and lax.ppermute only.
A program may use at most 256 MiB of HBM per device.

v0:
```python
import math
import jax
import jax.numpy as jnp
from jax import lax
from jax.sharding import PartitionSpec as P

HEADS = 16
HEAD_DIM = 128
STRETCH = 64
NEIGH = 2
CAP = 2


def shifted(value, axis, steps):
    count = lax.axis_size(axis)
    leading, last = (max(0, -steps), min(count, count - steps))
    return lax.ppermute(value, axis, [(source, source + steps) for source in range(leading, last)])


def normalize(values):
    wide = values.astype(jnp.float32)
    return (wide * lax.rsqrt(jnp.mean(wide * wide, axis=-1, keepdims=True) + 1e-06)).astype(
        jnp.bfloat16
    )


def shards(
    self_query,
    self_key,
    self_value,
    cross_query,
    retrieval_shard,
    retrieval_row,
    database,
    ffn_in,
    ffn_out,
    cross_projection,
):
    width = HEADS * HEAD_DIM
    scale = 1.0 / math.sqrt(HEAD_DIM)
    rows = self_query.shape[0]
    stretches = rows // STRETCH
    shard_list = retrieval_shard.reshape(-1)
    row_list = retrieval_row.reshape(-1)
    requests = shard_list.shape[0]
    owners = lax.axis_size("db")
    order = jnp.arange(requests)
    earlier = (order[:, None] > order[None, :]) & (shard_list[:, None] == shard_list[None, :])
    rank = jnp.sum(earlier.astype(jnp.int32), axis=1)
    slot = shard_list * CAP + rank
    slots = jnp.arange(owners * CAP)
    hits = slots[:, None] == slot[None, :]
    wanted = (jnp.sum(jnp.where(hits, row_list[None, :] + 1, 0), axis=1) - 1).reshape(owners, CAP)
    asked = lax.all_to_all(wanted, "db", split_axis=0, concat_axis=0, tiled=True)
    found = jnp.take(database, jnp.maximum(asked, 0), axis=0)
    found = jnp.where((asked >= 0)[:, :, None, None], found, jnp.zeros_like(found))
    arrived = lax.all_to_all(found, "db", split_axis=0, concat_axis=0, tiled=True)
    arrived = arrived.reshape(owners * CAP, arrived.shape[2], arrived.shape[3])
    picked = jnp.take(arrived, slot, axis=0)
    neighbours = picked.reshape(-1, picked.shape[2])
    span = NEIGH * arrived.shape[1]
    normed_in = normalize(neighbours)
    expanded = jax.nn.gelu(
        jnp.dot(
            normed_in,
            lax.all_gather(ffn_in, "db", axis=1, tiled=True),
            preferred_element_type=jnp.float32,
        ),
        approximate=True,
    ).astype(jnp.bfloat16)
    mixed = jnp.dot(
        expanded,
        lax.all_gather(ffn_out, "db", axis=0, tiled=True),
        preferred_element_type=jnp.float32,
    )
    encoded = (neighbours.astype(jnp.float32) + mixed).astype(jnp.bfloat16)
    normed_out = normalize(encoded)
    own = jnp.dot(
        normed_out,
        lax.all_gather(cross_projection, "db", axis=1, tiled=True),
        preferred_element_type=jnp.float32,
    ).astype(jnp.bfloat16)
    previous = shifted(own[-span:], "seq", 1)
    projected = jnp.concatenate([previous, own], axis=0)
    projected = projected.reshape(stretches + 1, span, 2, HEADS, HEAD_DIM)
    cross_keys = projected[:, :, 0]
    cross_values = projected[:, :, 1]
    padded = jnp.concatenate(
        [
            jnp.zeros((1, width), jnp.bfloat16),
            cross_query,
            jnp.zeros((STRETCH - 1, width), jnp.bfloat16),
        ],
        axis=0,
    )
    grouped_query = padded.reshape(stretches + 1, STRETCH, HEADS, HEAD_DIM)
    scores = (
        jnp.einsum("gqhd,gkhd->ghqk", grouped_query, cross_keys, preferred_element_type=jnp.float32)
        * scale
    )
    probs = jnp.exp(scores - jnp.max(scores, axis=-1, keepdims=True))
    denominator = jnp.sum(probs, axis=-1)
    cross_out = jnp.einsum(
        "ghqk,gkhd->gqhd",
        probs.astype(jnp.bfloat16),
        cross_values,
        preferred_element_type=jnp.float32,
    )
    cross_out = cross_out / jnp.transpose(denominator, (0, 2, 1))[..., None]
    cross_attended = cross_out.reshape(-1, width)[1 : rows + 1].astype(jnp.bfloat16)
    position = lax.axis_index("seq") * rows + jnp.arange(rows)
    query = self_query.reshape(rows, HEADS, HEAD_DIM)
    best = jnp.full((HEADS, rows), -1e30, jnp.float32)
    keys = lax.all_gather(self_key, "seq", axis=0, tiled=True).reshape(-1, HEADS, HEAD_DIM)
    values = lax.all_gather(self_value, "seq", axis=0, tiled=True).reshape(-1, HEADS, HEAD_DIM)
    count = keys.shape[0]
    block_scores = (
        jnp.einsum("qhd,khd->hqk", query, keys, preferred_element_type=jnp.float32) * scale
    )
    allowed = jnp.arange(count)[None, :] <= position[:, None]
    block_scores = jnp.where(allowed[None], block_scores, -1e30)
    fresh = jnp.maximum(best, jnp.max(block_scores, axis=-1))
    block_probs = jnp.where(allowed[None], jnp.exp(block_scores - fresh[..., None]), 0.0)
    running = jnp.sum(block_probs, axis=-1)
    summed = jnp.einsum(
        "hqk,khd->hqd", block_probs.astype(jnp.bfloat16), values, preferred_element_type=jnp.float32
    )
    best, running, summed = (fresh, running, summed)
    self_out = summed / running[..., None]
    self_attended = jnp.transpose(self_out, (1, 0, 2)).reshape(rows, width).astype(jnp.bfloat16)
    return (self_attended, cross_attended)


def solution(mesh):
    in_specs = (
        P(("db", "seq"), None),
        P(("db", "seq"), None),
        P(("db", "seq"), None),
        P(("db", "seq"), None),
        P(("db", "seq"), None),
        P(("db", "seq"), None),
        P("db", None, None),
        P(None, "db"),
        P("db", None),
        P(None, "db"),
    )
    out_specs = (P(("db", "seq"), None), P(("db", "seq"), None))
    return jax.shard_map(shards, mesh=mesh, in_specs=in_specs, out_specs=out_specs, check_vma=False)
```

profile of v0, /device:TPU:1, one launch (start us, length us, event | category | flops | bytes accessed | tf_op | source)
XLA Modules:
  0.0 461.4 jit_solution(2357627016175675936)
XLA Ops:
  7.2 0.0 all-gather.12.cloned.1.call-start
  7.2 0.7 all-gather.12.cloned.1.call-update
  7.9 0.0 all-gather.10.cloned.1.call-start
  8.0 0.7 all-gather.10.cloned.1.call-update
  8.7 0.0 all-gather.14.cloned.1.call-start
  8.7 0.7 all-gather.14.cloned.1.call-update
  9.4 0.0 all-gather.6.cloned.1.call-start
  9.5 2.6 copy.74
  12.0 0.0 all-gather.6.cloned.1.call-update
  12.1 0.1 copy.79
  12.2 0.1 add.102
  12.3 0.1 copy.78
  12.4 0.1 reshape.195
  12.4 0.2 convert_reduce_fusion
  12.6 0.1 select_reduce_fusion
  12.7 0.7 sub.25
  13.4 7.6 %all-to-all-start = ((s32[16,1,2]{2,1,0:T(1,128)}), s32[16,1,2]{2,1,0:T(1,128)S(1)}, u32[]{:S(2)}, u32[]{:S(2)}) async-start(s32[16,1,2]{2,1,0:T(1,128)} %bitcast.5), calls=%async_computation | async-start | bytes 16384 | tf_op jit(solution)/shard_map/all_to_all | solution.py:54
  21.0 0.0 all-gather.8.cloned.1.call-start
  21.1 0.5 all-gather.8.cloned.1.call-update
  21.6 5.7 %all-to-all-done = s32[16,1,2]{2,1,0:T(1,128)S(1)} async-done(((s32[16,1,2]{2,1,0:T(1,128)}), s32[16,1,2]{2,1,0:T(1,128)S(1)}, u32[]{:S(2)}, u32[]{:S(2)}) %all-to-all-start) | async-done | bytes 160 | tf_op jit(solution)/shard_map/all_to_all | solution.py:54
  27.4 0.1 copy.81
  27.5 0.1 copy.85
  27.5 0.1 reshape.202
  27.6 0.1 copy.84
  27.7 0.1 copy.82
  27.8 5.0 %gather_fusion = bf16[32,64,896]{2,1,0:T(8,128)(2,1)} fusion(bf16[32,64,896]{2,1,0:T(8,128)(2,1)} %param.16, s32[1024]{0:T(1024)S(1)} %pad_clamp_fusion.1), kind=kCustom, calls=%fused_computation | custom fusion | bytes 7340160 | tf_op jit(solution)/shard_map/jit(_take)/gather | solution.py:55
  32.8 4.5 select_select_fusion
  37.3 4.7 %all-to-all-start.1 = ((bf16[16,2,64,896]{3,2,1,0:T(8,128)(2,1)}), bf16[16,2,64,896]{3,2,1,0:T(8,128)(2,1)}, u32[]{:S(2)}, u32[]{:S(2)}) async-start(bf16[16,2,64,896]{3,2,1,0:T(8,128)(2,1)} %select_select_fusion), calls=%async_computation.1 | async-start | bytes 7340032 | tf_op jit(solution)/shard_map/all_to_all | solution.py:57
  42.0 0.1 copy.86
  42.1 0.1 mul.85
  42.2 0.1 broadcast_in_dim.97
  42.3 0.1 broadcast_in_dim.98
  42.4 0.1 pad.4.clone
  42.5 64.8 %all-to-all-done.1 = bf16[16,2,64,896]{3,2,1,0:T(8,128)(2,1)} async-done(((bf16[16,2,64,896]{3,2,1,0:T(8,128)(2,1)}), bf16[16,2,64,896]{3,2,1,0:T(8,128)(2,1)}, u32[]{:S(2)}, u32[]{:S(2)}) %all-to-all-start.1) | async-done | bytes 3670048 | tf_op jit(solution)/shard_map/all_to_all | solution.py:57
  107.3 2.8 gather_fusion.1
  110.1 0.5 multiply_reduce_fusion.1
  110.6 0.1 rsqrt.20
  110.7 1.4 bitcast_select_fusion
  112.1 66.4 %all-gather.10.cloned.1.call-done = bf16[896,3584]{0,1:T(8,128)(2,1)} async-done(((bf16[896,224]{0,1:T(8,128)(2,1)}), bf16[896,3584]{0,1:T(8,128)(2,1)}) %all-gather.10.cloned.1.call-update) | async-done | bytes 6422544 | tf_op jit(solution)/shard_map/all_gather | solution.py:66
  178.4 17.1 %fusion.24 = (f32[768]{0:T(1024)S(1)}, bf16[768,896]{1,0:T(8,128)(2,1)S(1)}) fusion(bf16[3584,896]{1,0:T(8,128)(2,1)} %all-gather.12.cloned.1.call-done, bf16[768,896]{1,0:T(8,128)(2,1)} %bitcast_select_fusion, bf16[896,3584]{0,1:T(8,128)(2,1)} %all-gather.10.cloned.1.call-done, f32[768]{0:T(1024)S(1)} %rsqrt.20), kind=kOutput, calls=%fused_computation.41 | convolution fusion | flops 9895967744 | bytes 15603712 | tf_op jit(solution)/shard_map/dot_general | solution.py:71
  195.6 56.7 %all-gather.14.cloned.1.call-done = bf16[896,4096]{1,0:T(8,128)(2,1)} async-done(((bf16[896,256]{1,0:T(8,128)(2,1)}), bf16[896,4096]{1,0:T(8,128)(2,1)}) %all-gather.14.cloned.1.call-update) | async-done | bytes 7340048 | tf_op jit(solution)/shard_map/all_gather | solution.py:80
  252.3 10.5 %convolution_convert_fusion = bf16[768,4096]{1,0:T(8,128)(2,1)S(1)} fusion(bf16[896,4096]{1,0:T(8,128)(2,1)} %all-gather.14.cloned.1.call-done, bf16[768,896]{1,0:T(8,128)(2,1)S(1)} %get-tuple-element.21, f32[768]{0:T(1024)S(1)} %add_rsqrt_fusion.1), kind=kOutput, calls=%fused_computation.19 | convolution fusion | flops 5642354688 | bytes 15010816 | tf_op jit(solution)/shard_map/dot_general | solution.py:78
  262.9 2.9 copy-done.2
  265.8 1.0 slice.21
  266.8 4.6 collective-permute-start
  271.4 0.8 maximum_bitcast_fusion.1
  272.3 1.8 copy.96
  274.0 0.7 iota_compare_fusion
  274.7 31.2 %collective-permute-done = bf16[128,4096]{1,0:T(8,128)(2,1)} collective-permute-done((bf16[128,4096]{1,0:T(8,128)(2,1)}, bf16[128,4096]{1,0:T(8,128)(2,1)}, u32[]{:S(2)}, u32[]{:S(2)}) %collective-permute-start) | collective-permute-done | bytes 1048608 | tf_op jit(solution)/shard_map/ppermute | solution.py:17
  305.9 6.9 %maximum_bitcast_fusion = bf16[112,8,32,128]{3,1,2,0:T(8,128)(2,1)} fusion(bf16[768,4096]{1,0:T(8,128)(2,1)} %copy-done.2, bf16[128,4096]{1,0:T(8,128)(2,1)} %collective-permute-done), kind=kLoop, calls=%fused_computation.18 | loop fusion | flops 14680064 | bytes 14680064
  312.8 5.5 %copy.97 = bf16[112,8,32,128]{3,2,1,0:T(8,128)(2,1)S(1)} copy(bf16[112,8,32,128]{3,1,2,0:T(8,128)(2,1)} %maximum_bitcast_fusion) | data formatting | bytes 14680064
  318.4 3.1 fusion.52
  321.4 2.7 multiply_reduce_fusion
  324.2 2.4 fusion.20
  326.6 2.5 fusion.18
  329.1 1.2 copy.90
  330.3 0.5 copy.118
  330.8 1.5 slice.24
  332.4 32.7 %fusion = (f32[16,384]{1,0:T(8,128)S(1)}, f32[16,384,3072]{2,1,0:T(8,128)}) fusion(pred[384,3072]{1,0:T(8,128)(4,1)S(1)} %iota_compare_fusion, bf16[3072,16,128]{0,2,1:T(8,128)(2,1)} %bitcast.73, bf16[384,2048]{1,0:T(8,128)(2,1)S(1)} %copy-done), kind=kOutput, calls=%fused_computation.4 | convolution fusion | flops 4888455168 | bytes 90857472 | tf_op jit(solution)/shard_map/qhd,khd->hqk/dot_general | solution.py:118
  365.0 25.9 %fusion.1 = f32[16,384]{1,0:T(8,128)S(1)} fusion(f32[16,384,3072]{2,1,0:T(8,128)} %get-tuple-element.19, f32[16,384]{1,0:T(8,128)S(1)} %broadcast_maximum_fusion, pred[384,3072]{1,0:T(8,128)(4,1)S(1)} %iota_compare_fusion), kind=kLoop, calls=%fused_computation.5 | loop fusion | flops 94365696 | bytes 76726272 | tf_op jit(solution)/shard_map/reduce_sum | solution.py:124
  391.0 10.8 %all-gather.8.cloned.1.call-done = bf16[3072,2048]{1,0:T(8,128)(2,1)} async-done(((bf16[384,2048]{1,0:T(8,128)(2,1)}), bf16[3072,2048]{1,0:T(8,128)(2,1)}) %all-gather.8.cloned.1.call-update) | async-done | bytes 12582928 | tf_op jit(solution)/shard_map/all_gather | solution.py:115
  401.8 16.6 %copy.77 = bf16[3072,2048]{0,1:T(8,128)(2,1)} copy(bf16[3072,2048]{1,0:T(8,128)(2,1)} %all-gather.8.cloned.1.call-done) | data formatting | bytes 25165824 | tf_op jit(solution)/shard_map/all_gather | solution.py:115
  418.4 33.8 %fusion.19 = bf16[384,16,128]{0,2,1:T(8,128)(2,1)} fusion(bf16[3072,16,128]{0,2,1:T(8,128)(2,1)} %bitcast.75, f32[16,384,3072]{2,1,0:T(8,128)} %get-tuple-element.19, f32[16,384]{1,0:T(8,128)S(1)} %broadcast_maximum_fusion, pred[384,3072]{1,0:T(8,128)(4,1)S(1)} %iota_compare_fusion, f32[384,16]{0,1:T(8,128)S(1)} %bitcast.81), kind=kOutput, calls=%fused_computation.36 | convolution fusion | flops 4927782912 | bytes 90882048 | tf_op jit(solution)/shard_map/hqk,khd->hqd/dot_general | solution.py:125
  452.3 2.6 copy.91
  (32 shorter events, 0.1 us)
Async XLA Ops:
  7.2 325.2 %copy-start = (bf16[384,2048]{1,0:T(8,128)(2,1)S(1)}, bf16[384,2048]{1,0:T(8,128)(2,1)}, u32[]{:S(2)}) copy-start(bf16[384,2048]{1,0:T(8,128)(2,1)} %param.10) | copy-start | bytes 4718596
  7.2 4.9 %copy-start.7 = (s32[6,2]{0,1:T(2,128)S(1)}, s32[6,2]{0,1:T(2,128)}, u32[]{:S(2)}) copy-start(s32[6,2]{0,1:T(2,128)} %param.15) | copy-start | bytes 148
  7.2 5.1 %copy-start.6 = (s32[6,2]{0,1:T(2,128)S(1)}, s32[6,2]{0,1:T(2,128)}, u32[]{:S(2)}) copy-start(s32[6,2]{0,1:T(2,128)} %param.14) | copy-start | bytes 148
  7.2 104.9 %all-gather.12.cloned.1.call-start = ((), (), s32[]{:S(2)}) async-start(), calls=%async_computation.5 | async-start | bytes 6823936 | tf_op jit(solution)/shard_map/all_gather | solution.py:73
  7.9 170.5 %all-gather.10.cloned.1.call-start = ((), (), s32[]{:S(2)}) async-start(), calls=%async_computation.4 | async-start | bytes 6823936 | tf_op jit(solution)/shard_map/all_gather | solution.py:66
  8.7 243.6 %all-gather.14.cloned.1.call-start = ((), (), s32[]{:S(2)}) async-start(), calls=%async_computation.6 | async-start | bytes 7798784 | tf_op jit(solution)/shard_map/all_gather | solution.py:80
  9.4 322.9 %all-gather.6.cloned.1.call-start = ((), (), s32[]{:S(2)}) async-start(), calls=%async_computation.2 | async-start | bytes 14155776 | tf_op jit(solution)/shard_map/all_gather | solution.py:114
  13.4 13.9 %all-to-all-start = ((s32[16,1,2]{2,1,0:T(1,128)}), s32[16,1,2]{2,1,0:T(1,128)S(1)}, u32[]{:S(2)}, u32[]{:S(2)}) async-start(s32[16,1,2]{2,1,0:T(1,128)} %bitcast.5), calls=%async_computation | async-start | bytes 16384 | tf_op jit(solution)/shard_map/all_to_all | solution.py:54
  21.0 380.7 %all-gather.8.cloned.1.call-start = ((), (), s32[]{:S(2)}) async-start(), calls=%async_computation.3 | async-start | bytes 14155776 | tf_op jit(solution)/shard_map/all_gather | solution.py:115
  37.3 70.0 %all-to-all-start.1 = ((bf16[16,2,64,896]{3,2,1,0:T(8,128)(2,1)}), bf16[16,2,64,896]{3,2,1,0:T(8,128)(2,1)}, u32[]{:S(2)}, u32[]{:S(2)}) async-start(bf16[16,2,64,896]{3,2,1,0:T(8,128)(2,1)} %select_select_fusion), calls=%async_computation.1 | async-start | bytes 7340032 | tf_op jit(solution)/shard_map/all_to_all | solution.py:57
  252.3 19.1 %copy-start.5 = (bf16[384,2048]{1,0:T(8,128)(2,1)S(1)}, bf16[384,2048]{1,0:T(8,128)(2,1)}, u32[]{:S(2)}) copy-start(bf16[384,2048]{1,0:T(8,128)(2,1)} %param.13) | copy-start | bytes 4718596
  262.8 2.9 copy-start.2
  266.8 39.1 %collective-permute-start = (bf16[128,4096]{1,0:T(8,128)(2,1)}, bf16[128,4096]{1,0:T(8,128)(2,1)}, u32[]{:S(2)}, u32[]{:S(2)}) collective-permute-start(bf16[128,4096]{1,0:T(8,128)(2,1)} %slice.21), channel_id=1, source_target_pairs={{0,1},{1,2},{2,3},{3,4},{4,5},{5,6},{6,7},{8,9},{9,10},{10,11},{11... | collective-permute-start | bytes 3145736 | tf_op jit(solution)/shard_map/ppermute | solution.py:17
  318.4 3.1 copy-start.3
  324.2 2.4 copy-start.4
  418.4 36.4 %copy-start.1 = (bf16[384,2048]{1,0:T(8,128)(2,1)S(1)}, bf16[384,2048]{1,0:T(8,128)(2,1)}, u32[]{:S(2)}) copy-start(bf16[384,2048]{1,0:T(8,128)(2,1)} %param.10) | copy-start | bytes 4718596
Sparse Core Ops, SparseCore 0:
  10.2 101.3 all-gather.11
  113.7 64.7 all-gather.9
  180.5 71.7 all-gather.13
  254.4 73.4 all-gather.5
  329.4 72.2 all-gather.7
where the time goes:
time: 462 us; the launch traced here: 461 us
  waiting for transfers between devices  238 us (52%)
  matrix products  99.4 us (22%)
  local copies, waits for them, and re-layouts  49.1 us (11%)
  other arithmetic  43.5 us (9%)
  starting transfers between devices  17.1 us (4%)
  between operations  14 us (3%)
    all_gather x1, waiting for transfers between devices, shards(): lax.all_gather(ffn_in, 'db', axis=1, tiled=True)  66.4 us
    all_to_all x1, waiting for transfers between devices, shards(): lax.all_to_all(found, 'db', split_axis=0, concat_axis=0, tiled=True)  64.8 us
    all_gather x1, waiting for transfers between devices, shards(): lax.all_gather(cross_projection, 'db', axis=1, tiled=True)  56.7 us
    dot_general x1, matrix products, shards(): jnp.einsum('hqk,khd->hqd', block_probs.astype(jnp.bfloat16), values, pref...  33.8 us
    dot_general x1, matrix products, shards(): jnp.einsum('qhd,khd->hqk', query, keys, preferred_element_type=jnp.float32)  32.7 us
    ppermute x1, waiting for transfers between devices, shifted(): lax.ppermute(value, axis, [(source, source + steps) for source in range(l...  31.2 us
    reduce_sum x1, other arithmetic, shards(): running = jnp.sum(block_probs, axis=-1)  25.9 us
    dot_general x1, matrix products, shards(): jnp.dot(expanded, lax.all_gather(ffn_out, 'db', axis=0, tiled=True), pref...  17.1 us
  transfers between devices with their start and end apart: 8, of which 6 were waited for; matrix products, arithmetic and copies ran while one was open for 29% of the time, Pallas kernels for 0%

commit v1 on v0

--- a/solution.py
+++ b/solution.py
@@ -9,6 +9,19 @@
 STRETCH = 64
 NEIGH = 2
 CAP = 2
+
+
+def gather_around(shard, axis, dim):
+    peers, here, extent = (lax.axis_size(axis), lax.axis_index(axis), shard.shape[dim])
+    right = [(i, (i + 1) % peers) for i in range(peers)]
+    whole = jnp.zeros((*shard.shape[:dim], peers * extent, *shard.shape[dim + 1 :]), shard.dtype)
+    held = shard
+    for hop in range(peers):
+        owner = (here - hop) % peers
+        whole = lax.dynamic_update_slice_in_dim(whole, held, owner * extent, axis=dim)
+        if hop < peers - 1:
+            held = lax.ppermute(held, axis, right)
+    return whole
 
 
 def shifted(value, axis, steps):
@@ -112,7 +125,7 @@
     query = self_query.reshape(rows, HEADS, HEAD_DIM)
     best = jnp.full((HEADS, rows), -1e30, jnp.float32)
     keys = lax.all_gather(self_key, "seq", axis=0, tiled=True).reshape(-1, HEADS, HEAD_DIM)
-    values = lax.all_gather(self_value, "seq", axis=0, tiled=True).reshape(-1, HEADS, HEAD_DIM)
+    values = gather_around(self_value, "seq", 0).reshape(-1, HEADS, HEAD_DIM)
     count = keys.shape[0]
     block_scores = (
         jnp.einsum("qhd,khd->hqk", query, keys, preferred_element_type=jnp.float32) * scale

time: 462 us -> 436 us (0.944); the launches traced: 461 us -> 429 us
  waiting for transfers between devices: 238 us -> 145 us
  local copies, waits for them, and re-layouts: 49.1 us -> 83.1 us
  blocking collectives: 0 us -> 13 us
  starting transfers between devices: 17.1 us -> 28.1 us
    all_gather x1, waiting for transfers between devices: 66.4 us -> 7.77 us  [shards(): lax.all_gather(ffn_in, 'db', axis=1, tiled=True)]
    all_to_all x1, waiting for transfers between devices: 64.8 us -> 17.2 us  [shards(): lax.all_to_all(found, 'db', split_axis=0, concat_axis=0, tiled=True)]
    ppermute x0 -> x7, waiting for transfers between devices: none -> 45.6 us  [gather_around(): held = lax.ppermute(held, axis, right)]
    dynamic_update_slice x0 -> x8, local copies, waits for them, and re-layouts: none -> 19.7 us  [gather_around(): lax.dynamic_update_slice_in_dim(whole, held, owner * extent, axis=dim)]
    ppermute x0 -> x7, local copies, waits for them, and re-layouts: none -> 18.5 us  [gather_around(): held = lax.ppermute(held, axis, right)]
    ppermute x0 -> x7, starting transfers between devices: none -> 16.8 us  [gather_around(): held = lax.ppermute(held, axis, right)]
    all_gather x1 -> x0, local copies, waits for them, and re-layouts: 16.6 us -> none  [shards(): lax.all_gather(self_value, 'seq', axis=0, tiled=True)]
    ppermute x1, waiting for transfers between devices: 31.2 us -> 17 us  [shifted(): lax.ppermute(value, axis, [(source, source + steps) for source in range(l...]
  transfers between devices with their start and end apart: 8 -> 13, of which waited for: 6 -> 8; matrix products, arithmetic and copies ran while one was open for 29% -> 30% of each run, Pallas kernels for 0% -> 0%
where the time goes in v1:
time: 436 us; the launch traced here: 429 us
  waiting for transfers between devices  145 us (33%)
  matrix products  99.1 us (23%)
  local copies, waits for them, and re-layouts  83.1 us (19%)
  other arithmetic  46.8 us (11%)
  starting transfers between devices  28.1 us (6%)
  between operations  14.2 us (3%)
  blocking collectives  13 us (3%)
    all_gather x1, waiting for transfers between devices, shards(): lax.all_gather(cross_projection, 'db', axis=1, tiled=True)  55.1 us
    ppermute x7, waiting for transfers between devices, gather_around(): held = lax.ppermute(held, axis, right)  45.6 us
    dot_general x1, matrix products, shards(): jnp.einsum('hqk,khd->hqd', block_probs.astype(jnp.bfloat16), values, pref...  33.8 us
    dot_general x1, matrix products, shards(): jnp.einsum('qhd,khd->hqk', query, keys, preferred_element_type=jnp.float32)  32.1 us
    reduce_sum x1, other arithmetic, shards(): running = jnp.sum(block_probs, axis=-1)  25.5 us
    unnamed x29, local copies, waits for them, and re-layouts  21.8 us
    dynamic_update_slice x8, local copies, waits for them, and re-layouts, gather_around(): lax.dynamic_update_slice_in_dim(whole, held, owner * extent, axis=dim)  19.7 us
    ppermute x7, local copies, waits for them, and re-layouts, gather_around(): held = lax.ppermute(held, axis, right)  18.5 us
  transfers between devices with their start and end apart: 13, of which 8 were waited for; matrix products, arithmetic and copies ran while one was open for 30% of the time, Pallas kernels for 0%

profile of v1, /device:TPU:1, one launch (start us, length us, event | category | flops | bytes accessed | tf_op | source)
XLA Modules:
  0.0 428.9 jit_solution(4938658335482337073)
XLA Ops:
  7.2 0.7 all-gather.9.cloned.1.call-update
  8.0 0.7 all-gather.7.cloned.1.call-update
  8.7 0.7 all-gather.11.cloned.1.call-update
  9.5 2.6 copy.102
  12.1 3.0 collective-permute-start
  15.1 17.7 %collective-permute-done = bf16[384,2048]{1,0:T(8,128)(2,1)S(1)} collective-permute-done((bf16[384,2048]{1,0:T(8,128)(2,1)}, bf16[384,2048]{1,0:T(8,128)(2,1)S(1)}, u32[]{:S(2)}, u32[]{:S(2)}) %collective-permute-start) | collective-permute-done | bytes 1572896 | tf_op jit(solution)/shard_map/ppermute | solution.py:23
  32.8 1.1 copy-done.8
  33.9 2.4 collective-permute-start.1
  36.3 17.4 %collective-permute-done.1 = bf16[384,2048]{1,0:T(8,128)(2,1)} collective-permute-done((bf16[384,2048]{1,0:T(8,128)(2,1)S(1)}, bf16[384,2048]{1,0:T(8,128)(2,1)}, u32[]{:S(2)}, u32[]{:S(2)}) %collective-permute-start.1) | collective-permute-done | bytes 1572896 | tf_op jit(solution)/shard_map/ppermute | solution.py:23
  53.7 2.6 collective-permute-start.2
  57.0 13.0 %all_to_all.11 = s32[16,1,2]{2,1,0:T(1,128)S(1)} all-to-all(s32[16,1,2]{2,1,0:T(1,128)S(1)} %bitcast.81), channel_id=1, replica_groups=mesh['db'=16,'seq'=8] {'db'}, dimensions={0} | all-to-all | bytes 256 | tf_op jit(solution)/shard_map/all_to_all | solution.py:67
  70.5 4.9 %gather_fusion = bf16[32,64,896]{2,1,0:T(8,128)(2,1)} fusion(bf16[32,64,896]{2,1,0:T(8,128)(2,1)} %param.16, s32[1024]{0:T(1024)S(1)} %pad_clamp_fusion.1), kind=kCustom, calls=%fused_computation | custom fusion | bytes 7340160 | tf_op jit(solution)/shard_map/jit(_take)/gather | solution.py:68
  75.4 1.4 collective-permute-start.3
  76.8 4.5 %select_select_fusion = bf16[16,2,64,896]{3,2,1,0:T(8,128)(2,1)} fusion(bf16[16,2,64,896]{3,2,1,0:T(8,128)(2,1)} %bitcast.74, pred[16,2]{1,0:T(8,128)(4,1)S(1)} %copy.119, pred[16,2]{1,0:T(8,128)(4,1)S(1)} %copy.117), kind=kLoop, calls=%fused_computation.29 | loop fusion | flops 3670016 | bytes 7340096 | tf_op jit(solution)/shard_map/jit(_where)/select_n | solution.py:69
  81.3 6.4 %all-to-all-start.1 = ((bf16[16,2,64,896]{3,2,1,0:T(8,128)(2,1)}), bf16[16,2,64,896]{3,2,1,0:T(8,128)(2,1)}, u32[]{:S(2)}, u32[]{:S(2)}) async-start(bf16[16,2,64,896]{3,2,1,0:T(8,128)(2,1)} %select_select_fusion), calls=%async_computation.1 | async-start | bytes 7340032 | tf_op jit(solution)/shard_map/all_to_all | solution.py:70
  87.7 2.7 copy.105
  90.6 3.8 collective-permute-done.3
  94.5 2.5 collective-permute-start.4
  97.0 6.2 %broadcast_in_dim.100 = bf16[3072,2048]{0,1:T(8,128)(2,1)} broadcast(bf16[]{:T(256)} %constant.113.clone.1), dimensions={} | broadcast | bytes 12582914 | tf_op jit(solution)/shard_map/broadcast_in_dim | solution.py:17
  103.1 1.5 constant_dynamic-update-slice_fusion.7
  105.1 2.1 maximum_bitcast_fusion.1
  107.2 0.7 iota_compare_fusion
  107.9 6.7 %collective-permute-done.4 = bf16[384,2048]{1,0:T(8,128)(2,1)} collective-permute-done((bf16[384,2048]{1,0:T(8,128)(2,1)}, bf16[384,2048]{1,0:T(8,128)(2,1)}, u32[]{:S(2)}, u32[]{:S(2)}) %collective-permute-start.4) | collective-permute-done | bytes 1572896 | tf_op jit(solution)/shard_map/ppermute | solution.py:23
  114.6 2.5 collective-permute-start.5
  117.3 3.3 copy.131
  120.6 2.6 copy.106
  123.1 2.8 constant_dynamic-update-slice_fusion.6
  126.0 2.6 copy.107
  128.6 2.7 constant_dynamic-update-slice_fusion.5
  131.3 17.2 %all-to-all-done.1 = bf16[16,2,64,896]{3,2,1,0:T(8,128)(2,1)} async-done(((bf16[16,2,64,896]{3,2,1,0:T(8,128)(2,1)}), bf16[16,2,64,896]{3,2,1,0:T(8,128)(2,1)}, u32[]{:S(2)}, u32[]{:S(2)}) %all-to-all-start.1) | async-done | bytes 3670048 | tf_op jit(solution)/shard_map/all_to_all | solution.py:70
  148.5 3.9 gather_fusion.1
  152.4 1.9 multiply_reduce_fusion.1
  154.4 2.7 bitcast_select_fusion
  157.1 2.6 copy.108
  159.7 2.9 constant_dynamic-update-slice_fusion.4
  162.6 3.0 copy.109
  165.6 2.4 collective-permute-start.6
  168.0 7.8 %all-gather.7.cloned.1.call-done = bf16[896,3584]{0,1:T(8,128)(2,1)} async-done(((bf16[896,224]{0,1:T(8,128)(2,1)}), bf16[896,3584]{0,1:T(8,128)(2,1)}) %all-gather.7.cloned.1.call-update) | async-done | bytes 6422544 | tf_op jit(solution)/shard_map/all_gather | solution.py:79
  175.8 18.1 %fusion.24 = (f32[768]{0:T(1024)S(1)}, bf16[768,896]{1,0:T(8,128)(2,1)}) fusion(bf16[3584,896]{1,0:T(8,128)(2,1)} %all-gather.9.cloned.1.call-done, bf16[768,896]{1,0:T(8,128)(2,1)} %bitcast_select_fusion, bf16[896,3584]{0,1:T(8,128)(2,1)} %all-gather.7.cloned.1.call-done, f32[768]{0:T(1024)S(1)} %rsqrt.20), kind=kOutput, calls=%fused_computation.41 | convolution fusion | flops 9895967744 | bytes 15603712 | tf_op jit(solution)/shard_map/dot_general | solution.py:84
  194.0 55.1 %all-gather.11.cloned.1.call-done = bf16[896,4096]{1,0:T(8,128)(2,1)} async-done(((bf16[896,256]{1,0:T(8,128)(2,1)}), bf16[896,4096]{1,0:T(8,128)(2,1)}) %all-gather.11.cloned.1.call-update) | async-done | bytes 7340048 | tf_op jit(solution)/shard_map/all_gather | solution.py:93
  249.1 9.7 %convolution_convert_fusion = bf16[768,4096]{1,0:T(8,128)(2,1)S(1)} fusion(bf16[896,4096]{1,0:T(8,128)(2,1)} %all-gather.11.cloned.1.call-done, bf16[768,896]{1,0:T(8,128)(2,1)} %get-tuple-element.21, f32[768]{0:T(1024)S(1)} %add_rsqrt_fusion.1), kind=kOutput, calls=%fused_computation.19 | convolution fusion | flops 5642354688 | bytes 15010816 | tf_op jit(solution)/shard_map/dot_general | solution.py:91
  258.8 2.9 copy-done.2
  261.7 1.0 slice.21
  262.8 4.6 %collective-permute-start.7 = (bf16[128,4096]{1,0:T(8,128)(2,1)}, bf16[128,4096]{1,0:T(8,128)(2,1)}, u32[]{:S(2)}, u32[]{:S(2)}) collective-permute-start(bf16[128,4096]{1,0:T(8,128)(2,1)} %slice.21), channel_id=1, source_target_pairs={{0,1},{1,2},{2,3},{3,4},{4,5},{5,6},{6,7},{8,9},{9,10},{10,11},{11... | collective-permute-start | bytes 3145736 | tf_op jit(solution)/shard_map/ppermute | solution.py:30
  267.4 1.4 constant_dynamic-update-slice_fusion.3
  268.8 2.6 copy.110
  271.4 2.8 constant_dynamic-update-slice_fusion.2
  274.2 2.6 copy.111
  276.7 2.8 constant_dynamic-update-slice_fusion.1
  279.5 2.6 copy.112
  282.1 2.8 constant_dynamic-update-slice_fusion
  284.9 17.0 %collective-permute-done.7 = bf16[128,4096]{1,0:T(8,128)(2,1)} collective-permute-done((bf16[128,4096]{1,0:T(8,128)(2,1)}, bf16[128,4096]{1,0:T(8,128)(2,1)}, u32[]{:S(2)}, u32[]{:S(2)}) %collective-permute-start.7) | collective-permute-done | bytes 1048608 | tf_op jit(solution)/shard_map/ppermute | solution.py:30
  301.9 6.9 %maximum_bitcast_fusion = bf16[112,8,32,128]{3,1,2,0:T(8,128)(2,1)} fusion(bf16[768,4096]{1,0:T(8,128)(2,1)} %copy-done.2, bf16[128,4096]{1,0:T(8,128)(2,1)} %collective-permute-done.7), kind=kLoop, calls=%fused_computation.18 | loop fusion | flops 14680064 | bytes 14680064
  308.8 5.5 %copy.132 = bf16[112,8,32,128]{3,2,1,0:T(8,128)(2,1)S(1)} copy(bf16[112,8,32,128]{3,1,2,0:T(8,128)(2,1)} %maximum_bitcast_fusion) | data formatting | bytes 14680064
  314.4 3.1 fusion.52
  317.4 2.7 multiply_reduce_fusion
  320.1 2.1 fusion.20
  322.3 2.5 fusion.18
  324.8 1.2 copy.125
  326.5 1.5 slice.24
  328.1 32.1 %fusion = (f32[16,384]{1,0:T(8,128)S(1)}, f32[16,384,3072]{2,1,0:T(8,128)}) fusion(pred[384,3072]{1,0:T(8,128)(4,1)S(1)} %iota_compare_fusion, bf16[3072,16,128]{0,2,1:T(8,128)(2,1)} %bitcast.73, bf16[384,2048]{1,0:T(8,128)(2,1)S(1)} %copy-done), kind=kOutput, calls=%fused_computation.4 | convolution fusion | flops 4888455168 | bytes 90857472 | tf_op jit(solution)/shard_map/qhd,khd->hqk/dot_general | solution.py:131
  360.2 25.5 %fusion.1 = f32[16,384]{1,0:T(8,128)S(1)} fusion(f32[16,384,3072]{2,1,0:T(8,128)} %get-tuple-element.19, f32[16,384]{1,0:T(8,128)S(1)} %broadcast_maximum_fusion, pred[384,3072]{1,0:T(8,128)(4,1)S(1)} %iota_compare_fusion), kind=kLoop, calls=%fused_computation.5 | loop fusion | flops 94365696 | bytes 76726272 | tf_op jit(solution)/shard_map/reduce_sum | solution.py:137
  385.7 33.8 %fusion.19 = bf16[384,16,128]{0,2,1:T(8,128)(2,1)} fusion(bf16[3072,16,128]{0,2,1:T(8,128)(2,1)} %bitcast.75, f32[16,384,3072]{2,1,0:T(8,128)} %get-tuple-element.19, f32[16,384]{1,0:T(8,128)S(1)} %broadcast_maximum_fusion, pred[384,3072]{1,0:T(8,128)(4,1)S(1)} %iota_compare_fusion, f32[384,16]{0,1:T(8,128)S(1)} %bitcast.82), kind=kOutput, calls=%fused_computation.36 | convolution fusion | flops 4927782912 | bytes 90882048 | tf_op jit(solution)/shard_map/hqk,khd->hqd/dot_general | solution.py:138
  419.6 2.6 copy.126
  (64 shorter events, 2.9 us)
Async XLA Ops:
  7.2 320.9 %copy-start = (bf16[384,2048]{1,0:T(8,128)(2,1)S(1)}, bf16[384,2048]{1,0:T(8,128)(2,1)}, u32[]{:S(2)}) copy-start(bf16[384,2048]{1,0:T(8,128)(2,1)} %param.10) | copy-start | bytes 4718596
  7.2 49.1 %copy-start.10 = (s32[6,2]{0,1:T(2,128)S(1)}, s32[6,2]{0,1:T(2,128)}, u32[]{:S(2)}) copy-start(s32[6,2]{0,1:T(2,128)} %param.15) | copy-start | bytes 148
  7.2 49.3 %copy-start.9 = (s32[6,2]{0,1:T(2,128)S(1)}, s32[6,2]{0,1:T(2,128)}, u32[]{:S(2)}) copy-start(s32[6,2]{0,1:T(2,128)} %param.14) | copy-start | bytes 148
  7.2 160.8 %all-gather.9.cloned.1.call-start = ((), (), s32[]{:S(2)}) async-start(), calls=%async_computation.4 | async-start | bytes 6823936 | tf_op jit(solution)/shard_map/all_gather | solution.py:86
  7.9 167.9 %all-gather.7.cloned.1.call-start = ((), (), s32[]{:S(2)}) async-start(), calls=%async_computation.3 | async-start | bytes 6823936 | tf_op jit(solution)/shard_map/all_gather | solution.py:79
  8.7 240.4 %all-gather.11.cloned.1.call-start = ((), (), s32[]{:S(2)}) async-start(), calls=%async_computation.5 | async-start | bytes 7798784 | tf_op jit(solution)/shard_map/all_gather | solution.py:93
  9.4 318.6 %all-gather.5.cloned.1.call-start = ((), (), s32[]{:S(2)}) async-start(), calls=%async_computation.2 | async-start | bytes 14155776 | tf_op jit(solution)/shard_map/all_gather | solution.py:127
  12.1 20.7 %collective-permute-start = (bf16[384,2048]{1,0:T(8,128)(2,1)}, bf16[384,2048]{1,0:T(8,128)(2,1)S(1)}, u32[]{:S(2)}, u32[]{:S(2)}) collective-permute-start(bf16[384,2048]{1,0:T(8,128)(2,1)} %param.12), channel_id=1, source_target_pairs={{0,1},{1,2},{2,3},{3,4},{4,5},{5,6},{6,7},{7,0},{8,9},{9,10},{10,1... | collective-permute-start | bytes 4718600 | tf_op jit(solution)/shard_map/ppermute | solution.py:23
  32.8 1.1 copy-start.8
  33.9 19.7 %collective-permute-start.1 = (bf16[384,2048]{1,0:T(8,128)(2,1)S(1)}, bf16[384,2048]{1,0:T(8,128)(2,1)}, u32[]{:S(2)}, u32[]{:S(2)}) collective-permute-start(bf16[384,2048]{1,0:T(8,128)(2,1)S(1)} %collective-permute-done), channel_id=1, source_target_pairs={{0,1},{1,2},{2,3},{3,4},{4,5},{5,6},{6,7},{7,0},{8,9},{9,10},{10,1... | collective-permute-start | bytes 4718600 | tf_op jit(solution)/shard_map/ppermute | solution.py:23
  53.7 21.7 %collective-permute-start.2 = (bf16[384,2048]{1,0:T(8,128)(2,1)}, bf16[384,2048]{1,0:T(8,128)(2,1)}, u32[]{:S(2)}, u32[]{:S(2)}) collective-permute-start(bf16[384,2048]{1,0:T(8,128)(2,1)} %collective-permute-done.1), channel_id=1, source_target_pairs={{0,1},{1,2},{2,3},{3,4},{4,5},{5,6},{6,7},{7,0},{8,9},{9,10},{10,1... | collective-permute-start | bytes 4718600 | tf_op jit(solution)/shard_map/ppermute | solution.py:23
  75.4 19.1 %collective-permute-start.3 = (bf16[384,2048]{1,0:T(8,128)(2,1)}, bf16[384,2048]{1,0:T(8,128)(2,1)}, u32[]{:S(2)}, u32[]{:S(2)}) collective-permute-start(bf16[384,2048]{1,0:T(8,128)(2,1)} %collective-permute-done.2), channel_id=1, source_target_pairs={{0,1},{1,2},{2,3},{3,4},{4,5},{5,6},{6,7},{7,0},{8,9},{9,10},{10,1... | collective-permute-start | bytes 4718600 | tf_op jit(solution)/shard_map/ppermute | solution.py:23
  81.3 67.3 %all-to-all-start.1 = ((bf16[16,2,64,896]{3,2,1,0:T(8,128)(2,1)}), bf16[16,2,64,896]{3,2,1,0:T(8,128)(2,1)}, u32[]{:S(2)}, u32[]{:S(2)}) async-start(bf16[16,2,64,896]{3,2,1,0:T(8,128)(2,1)} %select_select_fusion), calls=%async_computation.1 | async-start | bytes 7340032 | tf_op jit(solution)/shard_map/all_to_all | solution.py:70
  94.5 20.2 %collective-permute-start.4 = (bf16[384,2048]{1,0:T(8,128)(2,1)}, bf16[384,2048]{1,0:T(8,128)(2,1)}, u32[]{:S(2)}, u32[]{:S(2)}) collective-permute-start(bf16[384,2048]{1,0:T(8,128)(2,1)} %collective-permute-done.3), channel_id=1, source_target_pairs={{0,1},{1,2},{2,3},{3,4},{4,5},{5,6},{6,7},{7,0},{8,9},{9,10},{10,1... | collective-permute-start | bytes 4718600 | tf_op jit(solution)/shard_map/ppermute | solution.py:23
  97.0 6.2 %copy-start.4 = (bf16[384,2048]{0,1:T(8,128)(2,1)S(1)}, bf16[384,2048]{0,1:T(8,128)(2,1)}, u32[]{:S(2)}) copy-start(bf16[384,2048]{0,1:T(8,128)(2,1)} %copy.105) | copy-start | bytes 4718596
  103.1 2.0 copy-start.7
  114.6 50.9 %collective-permute-start.5 = (bf16[384,2048]{1,0:T(8,128)(2,1)}, bf16[384,2048]{1,0:T(8,128)(2,1)}, u32[]{:S(2)}, u32[]{:S(2)}) collective-permute-start(bf16[384,2048]{1,0:T(8,128)(2,1)} %collective-permute-done.4), channel_id=1, source_target_pairs={{0,1},{1,2},{2,3},{3,4},{4,5},{5,6},{6,7},{7,0},{8,9},{9,10},{10,1... | collective-permute-start | bytes 4718600 | tf_op jit(solution)/shard_map/ppermute | solution.py:23
  165.6 114.0 %collective-permute-start.6 = (bf16[384,2048]{1,0:T(8,128)(2,1)}, bf16[384,2048]{1,0:T(8,128)(2,1)}, u32[]{:S(2)}, u32[]{:S(2)}) collective-permute-start(bf16[384,2048]{1,0:T(8,128)(2,1)} %collective-permute-done.5), channel_id=1, source_target_pairs={{0,1},{1,2},{2,3},{3,4},{4,5},{5,6},{6,7},{7,0},{8,9},{9,10},{10,1... | collective-permute-start | bytes 4718600 | tf_op jit(solution)/shard_map/ppermute | solution.py:23
  249.1 18.4 %copy-start.5 = (bf16[384,2048]{0,1:T(8,128)(2,1)S(1)}, bf16[384,2048]{0,1:T(8,128)(2,1)}, u32[]{:S(2)}) copy-start(bf16[384,2048]{0,1:T(8,128)(2,1)} %copy.109) | copy-start | bytes 4718596
  258.8 3.0 copy-start.2
  262.8 39.1 %collective-permute-start.7 = (bf16[128,4096]{1,0:T(8,128)(2,1)}, bf16[128,4096]{1,0:T(8,128)(2,1)}, u32[]{:S(2)}, u32[]{:S(2)}) collective-permute-start(bf16[128,4096]{1,0:T(8,128)(2,1)} %slice.21), channel_id=1, source_target_pairs={{0,1},{1,2},{2,3},{3,4},{4,5},{5,6},{6,7},{8,9},{9,10},{10,11},{11... | collective-permute-start | bytes 3145736 | tf_op jit(solution)/shard_map/ppermute | solution.py:30
  314.3 3.1 copy-start.3
  320.1 2.2 copy-start.6
  385.7 36.4 %copy-start.1 = (bf16[384,2048]{1,0:T(8,128)(2,1)S(1)}, bf16[384,2048]{1,0:T(8,128)(2,1)}, u32[]{:S(2)}) copy-start(bf16[384,2048]{1,0:T(8,128)(2,1)} %param.10) | copy-start | bytes 4718596
Sparse Core Ops, SparseCore 0:
  10.2 64.9 all-gather.8
  77.3 98.4 all-gather.6
  177.9 71.0 all-gather.10
  250.6 73.4 all-gather.4
